TPU v7x, 32 devices: a whole 2x2x4 slice. The times are simulated.
32 devices in a mesh: groups: 2 (over y), ctx: 4 (over z), head: 2 (over x), rep: 2 (over core).
Axes of the slice: x: 2, y: 2, z: 4, core: 2. Of those that a mesh axis runs over, the one named last changes fastest.
Arguments:
- queries: bfloat16 [4, 512, 1024], P(('groups', 'rep'), 'ctx', 'head'), parts along dimension 0, may hold values from -6 to 6
- per_head_keys: bfloat16 [4, 512, 1024], P(('groups', 'rep'), 'ctx', 'head'), parts along dimension 0, may hold values from -6 to 6
- value_rows: bfloat16 [4, 512, 1024], P(('groups', 'rep'), 'ctx', 'head'), parts along dimension 0, may hold values from -6 to 6
- gate_logits: bfloat16 [4, 512, 1024], P(('groups', 'rep'), 'ctx', 'head'), parts along dimension 0, may hold values from -16 to 4
- gate_bias: float32 [1024], P('head'), may hold values from -1 to 13
- value_weight: float32 [1024], P('head'), may hold values from -0.1875 to 0.1875
- targets: float32 [4, 512], P(('groups', 'rep'), 'ctx'), parts along dimension 0, may hold values from -6 to 6
- mask_ids: int32 [4, 4], P(('groups', 'rep'), 'ctx'), parts along dimension 0, may hold values from 0 to 3
- segment_starts: int32 [4, 512], P(('groups', 'rep'), 'ctx'), parts along dimension 0, may hold values 0 or 1
Outputs:
- value_pred: float32 [4, 512], P(('groups', 'rep'), 'ctx'), parts along dimension 0
- query_gradient_rows: bfloat16 [4, 512, 1024], P(('groups', 'rep'), 'ctx', 'head'), parts along dimension 0
- grad_keys: bfloat16 [4, 512, 1024], P(('groups', 'rep'), 'ctx', 'head'), parts along dimension 0
- grad_values: bfloat16 [4, 512, 1024], P(('groups', 'rep'), 'ctx', 'head'), parts along dimension 0
- grad_gate_logits: bfloat16 [4, 512, 1024], P(('groups', 'rep'), 'ctx', 'head'), parts along dimension 0
- grad_gate_bias: float32 [2048], P(('groups', 'head')), parts along dimension 0
- grad_value_weight: float32 [2048], P(('groups', 'head')), parts along dimension 0
There are 2 independent parts, one for each index of `groups`. A program takes and returns all parts, laid end to end along the dimension named above; an argument that names none is the same for every part. Nothing has to cross between parts.
Inputs may be any that keep to these rules, and one draw needn't show every extreme that they name: `mask_ids`: the window kind of each block of 128 positions. `segment_starts`: flags of segment starts.
All inputs are finite; a program needn't handle non-finite values. No bound on the sum of `segment_starts` on one device may be relied on, other than what follows from the above.
Results may differ from a plain program's by a relative error of at most 0.013.
Values sent between devices are 32-bit elements; how exact they have to be, the bound alone decides.
A program may use at most 64 MiB of HBM per device.

v0:
```python
import jax
import jax.numpy as jnp
from jax import lax
from jax.sharding import PartitionSpec as P

DK = 128
DV = 128


epsilon = 1.0
gate_scale = 16.0
highest = lax.Precision.HIGHEST


def from_behind(value, axis, by):
    length = lax.axis_size(axis)
    pairs = [(i, i + by) for i in range(length) if 0 <= i + by < length]
    return lax.ppermute(value, axis, pairs)


def block_pass(query_in, key_in, value_in, decay, start_flags, kind_ids):
    blocks = kind_ids.shape[0]
    block_len = query_in.shape[0] // blocks
    head_count = query_in.shape[1]
    channels = query_in.shape[2]
    value_width = value_in.shape[2]
    query_f = query_in.astype(jnp.float32).reshape(blocks, block_len, head_count, channels)
    key_f = key_in.astype(jnp.float32).reshape(blocks, block_len, head_count, channels)
    value_bf = value_in.reshape(blocks, block_len, head_count, value_width)
    value_f = value_bf.astype(jnp.float32)
    log_cum = jnp.cumsum(decay.reshape(blocks, block_len, head_count, channels), axis=1)
    log_last = log_cum[:, -1]
    segment = jnp.cumsum(start_flags.reshape(blocks, block_len), axis=1, dtype=jnp.int32)
    alive_mask = (segment == 0).astype(jnp.float32)
    offsets = jnp.arange(block_len, dtype=jnp.int32)
    distance = offsets[:, None] - offsets[None, :]
    window = block_len // jnp.left_shift(jnp.ones_like(kind_ids), kind_ids)
    live_pairs = (
        (segment[:, :, None] == segment[:, None, :])
        & (distance[None] >= 0)
        & (distance[None] < window[:, None, None])
    )
    query_dec = query_f * jnp.exp(log_cum) * channels ** (-0.5)
    key_dec = key_f * jnp.exp(-log_cum)
    scores = jnp.einsum("bihc,bjhc->bhij", query_dec, key_dec, precision=highest)
    block_probs = jnp.where(live_pairs[:, None], scores, 0.0).astype(jnp.bfloat16)
    inner_part = jnp.einsum(
        "bhij,bjhd->bihd", block_probs, value_bf, preferred_element_type=jnp.float32
    )
    tail_mask = (segment == segment[:, -1:]).astype(jnp.float32)
    key_tail = key_f * jnp.exp(log_last[:, None] - log_cum) * tail_mask[:, :, None, None]
    block_state = jnp.einsum("bjhc,bjhd->bhcd", key_tail, value_f, precision=highest)
    block_decay = jnp.exp(log_last) * alive_mask[:, -1][:, None, None]

    def advance(carried_in, block_items):
        state_now, factor = carried_in
        new_state = state_now * block_items[1][..., None] + block_items[0]
        return ((new_state, factor * block_items[1]), (state_now, factor))

    initial = (
        jnp.zeros((head_count, channels, value_width), jnp.float32),
        jnp.ones((head_count, channels), jnp.float32),
    )
    finals, befores = lax.scan(advance, initial, (block_state, block_decay))
    query_live = query_dec * alive_mask[:, :, None, None]
    outer_part = jnp.einsum("bihc,bhcd->bihd", query_live, befores[0], precision=highest)
    carried = query_live * befores[1][:, None]
    attended = (inner_part + outer_part).reshape(blocks * block_len, head_count, value_width)
    return (
        attended,
        finals[0],
        finals[1],
        carried.reshape(blocks * block_len, head_count, channels),
    )


def on_device(
    queries,
    per_head_keys,
    value_rows,
    gate_logits,
    gate_bias,
    value_weight,
    targets,
    mask_ids,
    segment_starts,
):
    token_count = queries.shape[1]
    head_count = gate_bias.shape[0] // DK

    def to_heads(array):
        return array[0].reshape(token_count, head_count, -1)

    start_flags = segment_starts[0]
    kind_ids = mask_ids[0]

    def local_terms(query_in, key_in, value_in, logit_in, bias_in):
        decay = jax.nn.log_sigmoid(logit_in.astype(jnp.float32) + bias_in) / gate_scale
        return block_pass(query_in, key_in, value_in, decay, start_flags, kind_ids)

    local_out, pull_local = jax.vjp(
        local_terms,
        to_heads(queries),
        to_heads(per_head_keys),
        to_heads(value_rows),
        to_heads(gate_logits),
        gate_bias.reshape(head_count, DK),
    )
    attended_local, state_local, decay_local, carried = local_out

    def pass_state(position, incoming):
        return from_behind(incoming * decay_local[..., None] + state_local, "ctx", 1)

    state_in = lax.fori_loop(0, lax.axis_size("ctx") - 1, pass_state, jnp.zeros_like(state_local))
    attended = attended_local + jnp.einsum("thc,hcd->thd", carried, state_in, precision=highest)

    def value_head(attended_in, weight_in):
        normed = attended_in * lax.rsqrt(
            jnp.mean(attended_in * attended_in, axis=-1, keepdims=True) + epsilon
        )
        return jnp.einsum("thd,hd->t", normed, weight_in, precision=highest)

    partial_value, pull_value = jax.vjp(value_head, attended, value_weight.reshape(head_count, DV))
    value_pred = lax.psum(partial_value, "head")
    residual = value_pred - targets[0]
    grad_attended, grad_weight = pull_value(residual)
    grad_carried = jnp.einsum("thd,hcd->thc", grad_attended, state_in, precision=highest)
    grad_direct = jnp.einsum("thc,thd->hcd", carried, grad_attended, precision=highest)

    def pass_grad(position, incoming):
        return from_behind(grad_direct + decay_local[..., None] * incoming, "ctx", -1)

    grad_state = lax.fori_loop(0, lax.axis_size("ctx") - 1, pass_grad, jnp.zeros_like(grad_direct))
    grad_decay = jnp.sum(state_in * grad_state, axis=-1)
    grad_query, grad_key, grad_value, grad_logit, grad_bias = pull_local(
        (grad_attended, grad_state, grad_decay, grad_carried)
    )
    token_total = token_count * lax.axis_size("ctx") * lax.axis_size("rep")
    bias_total, weight_total = lax.psum(
        (grad_bias.reshape(-1), grad_weight.reshape(-1)), ("ctx", "rep")
    )
    return (
        value_pred[None],
        grad_query.reshape(1, token_count, -1),
        grad_key.reshape(1, token_count, -1),
        grad_value.reshape(1, token_count, -1),
        grad_logit.reshape(1, token_count, -1),
        bias_total / token_total,
        weight_total / token_total,
    )


def solution(mesh):
    in_specs = (
        P(("groups", "rep"), "ctx", "head"),
        P(("groups", "rep"), "ctx", "head"),
        P(("groups", "rep"), "ctx", "head"),
        P(("groups", "rep"), "ctx", "head"),
        P("head"),
        P("head"),
        P(("groups", "rep"), "ctx"),
        P(("groups", "rep"), "ctx"),
        P(("groups", "rep"), "ctx"),
    )
    out_specs = (
        P(("groups", "rep"), "ctx"),
        P(("groups", "rep"), "ctx", "head"),
        P(("groups", "rep"), "ctx", "head"),
        P(("groups", "rep"), "ctx", "head"),
        P(("groups", "rep"), "ctx", "head"),
        P(("groups", "head")),
        P(("groups", "head")),
    )
    return jax.shard_map(
        on_device, mesh=mesh, in_specs=in_specs, out_specs=out_specs, check_vma=False
    )
```

profile of v0, /device:TPU:0, one launch (start us, length us, event | category | flops | bytes accessed | tf_op | source)
XLA Modules:
  0.0 105.6 jit_solution(13447743507898511805)
XLA Ops:
  0.6 1.0 reshape.486
  1.7 0.4 fusion.9
  2.0 0.6 copy-done.13
  2.7 0.3 reduce_window_sum.35
  3.0 0.6 slice.11
  4.2 0.6 slice.12
  4.8 1.2 %compare_convert_fusion.1 = (f32[128]{0:T(128)}, f32[128]{0:T(128)S(1)}) fusion(s32[1,128]{1,0:T(1,128)S(1)} %reduce_window_sum.35, s32[]{:T(128)} %bitcast.14), kind=kLoop, calls=%fused_computation.129 | loop fusion | flops 512 | bytes 1540 | tf_op jit(solution)/shard_map/jvp()/convert_element_type | solution.py:34
  6.3 0.8 copy-done.2
  7.1 0.5 convolution_add_fusion
  7.6 28.2 %while.4 = (s32[]{:T(128)}, f32[4,128,128]{2,1,0:T(8,128)S(1)}, f32[4,128]{1,0:T(4,128)S(1)}, f32[4,128,128]{2,1,0:T(8,128)S(1)}, s32[]{:T(128)}) while((s32[]{:T(128)}, f32[4,128,128]{2,1,0:T(8,128)S(1)}, f32[4,128]{1,0:T(4,128)S(1)}, f32[4,128,128]{2,1,0:T(8,128)S(1)}, s32[]{:T(128)}) %tuple.61), condition=%wide.region_3.4_spmd, body=%wide.region_2.3_spmd.sunk | while | flops 131074 | bytes 1837157 | solution.py:114
  7.6 0.1 multiply_add_fusion.5
  7.8 4.9 %collective-permute-start = (f32[4,128,128]{2,1,0:T(8,128)S(1)}, f32[4,128,128]{2,1,0:T(8,128)S(1)}, u32[]{:S(2)}, u32[]{:S(2)}) collective-permute-start(f32[4,128,128]{2,1,0:T(8,128)S(1)} %multiply_add_fusion.5), channel_id=1, source_target_pairs={{0,4},{4,8},{8,12},{1,5},{5,9},{9,13},{2,6},{6,10},{10,14},{3,7},{... | collective-permute-start | bytes 786440 | tf_op jit(solution)/shard_map/while/body/eval_jaxpr/ppermute | solution.py:18
  12.7 5.5 %collective-permute-done = f32[4,128,128]{2,1,0:T(8,128)S(1)} collective-permute-done((f32[4,128,128]{2,1,0:T(8,128)S(1)}, f32[4,128,128]{2,1,0:T(8,128)S(1)}, u32[]{:S(2)}, u32[]{:S(2)}) %collective-permute-start) | collective-permute-done | bytes 262176 | tf_op jit(solution)/shard_map/while/body/eval_jaxpr/ppermute | solution.py:18
  18.4 4.4 %collective-permute-start = (f32[4,128,128]{2,1,0:T(8,128)S(1)}, f32[4,128,128]{2,1,0:T(8,128)S(1)}, u32[]{:S(2)}, u32[]{:S(2)}) collective-permute-start(f32[4,128,128]{2,1,0:T(8,128)S(1)} %multiply_add_fusion.5), channel_id=1, source_target_pairs={{0,4},{4,8},{8,12},{1,5},{5,9},{9,13},{2,6},{6,10},{10,14},{3,7},{... | collective-permute-start | bytes 786440 | tf_op jit(solution)/shard_map/while/body/eval_jaxpr/ppermute | solution.py:18
  22.8 4.7 %collective-permute-done = f32[4,128,128]{2,1,0:T(8,128)S(1)} collective-permute-done((f32[4,128,128]{2,1,0:T(8,128)S(1)}, f32[4,128,128]{2,1,0:T(8,128)S(1)}, u32[]{:S(2)}, u32[]{:S(2)}) %collective-permute-start) | collective-permute-done | bytes 262176 | tf_op jit(solution)/shard_map/while/body/eval_jaxpr/ppermute | solution.py:18
  27.6 4.4 %collective-permute-start = (f32[4,128,128]{2,1,0:T(8,128)S(1)}, f32[4,128,128]{2,1,0:T(8,128)S(1)}, u32[]{:S(2)}, u32[]{:S(2)}) collective-permute-start(f32[4,128,128]{2,1,0:T(8,128)S(1)} %multiply_add_fusion.5), channel_id=1, source_target_pairs={{0,4},{4,8},{8,12},{1,5},{5,9},{9,13},{2,6},{6,10},{10,14},{3,7},{... | collective-permute-start | bytes 786440 | tf_op jit(solution)/shard_map/while/body/eval_jaxpr/ppermute | solution.py:18
  32.0 3.9 %collective-permute-done = f32[4,128,128]{2,1,0:T(8,128)S(1)} collective-permute-done((f32[4,128,128]{2,1,0:T(8,128)S(1)}, f32[4,128,128]{2,1,0:T(8,128)S(1)}, u32[]{:S(2)}, u32[]{:S(2)}) %collective-permute-start) | collective-permute-done | bytes 262176 | tf_op jit(solution)/shard_map/while/body/eval_jaxpr/ppermute | solution.py:18
  37.0 0.7 fusion.2
  37.7 0.2 convolution_bitcast_fusion.1
  37.9 0.7 fusion.1
  38.6 0.7 multiply_reduce_fusion.2
  39.4 0.6 copy-done.4
  40.0 0.2 convolution_bitcast_fusion.2
  40.3 4.9 %psum.21 = f32[128]{0:T(128)S(1)} all-reduce(f32[128]{0:T(128)S(1)} %convolution_bitcast_fusion.2), channel_id=1, replica_groups=mesh['groups'=2,'ctx'=4,'head'=2,'rep'=2] {'head'}, use_global_device_ids=true, to_apply=%region_5.6 | all-reduce | flops 128 | bytes 1024 | tf_op jit(solution)/shard_map/psum | solution.py:124
  45.2 0.5 copy-done.15
  45.7 0.1 fusion.6
  45.9 0.7 fusion.60
  46.6 28.3 %while.5 = (s32[]{:T(128)}, f32[4,128,128]{2,1,0:T(8,128)S(1)}, f32[4,128]{1,0:T(4,128)S(1)}, f32[4,128,128]{2,1,0:T(8,128)S(1)}, s32[]{:T(128)}) while((s32[]{:T(128)}, f32[4,128,128]{2,1,0:T(8,128)S(1)}, f32[4,128]{1,0:T(4,128)S(1)}, f32[4,128,128]{2,1,0:T(8,128)S(1)}, s32[]{:T(128)}) %tuple.67), condition=%wide.region_8.9_spmd, body=%wide.region_7.8_spmd.sunk | while | flops 131074 | bytes 1837157 | solution.py:133
  46.6 0.1 multiply_add_fusion.6
  46.8 1.3 %collective-permute-start.1 = (f32[4,128,128]{2,1,0:T(8,128)S(1)}, f32[4,128,128]{2,1,0:T(8,128)S(1)}, u32[]{:S(2)}, u32[]{:S(2)}) collective-permute-start(f32[4,128,128]{2,1,0:T(8,128)S(1)} %multiply_add_fusion.6), channel_id=1, source_target_pairs={{4,0},{8,4},{12,8},{5,1},{9,5},{13,9},{6,2},{10,6},{14,10},{7,3},{... | collective-permute-start | bytes 786440 | tf_op jit(solution)/shard_map/while/body/eval_jaxpr/ppermute | solution.py:18
  48.1 7.9 %collective-permute-done.1 = f32[4,128,128]{2,1,0:T(8,128)S(1)} collective-permute-done((f32[4,128,128]{2,1,0:T(8,128)S(1)}, f32[4,128,128]{2,1,0:T(8,128)S(1)}, u32[]{:S(2)}, u32[]{:S(2)}) %collective-permute-start.1) | collective-permute-done | bytes 262176 | tf_op jit(solution)/shard_map/while/body/eval_jaxpr/ppermute | solution.py:18
  55.9 0.1 multiply_add_fusion.6
  56.1 1.3 %collective-permute-start.1 = (f32[4,128,128]{2,1,0:T(8,128)S(1)}, f32[4,128,128]{2,1,0:T(8,128)S(1)}, u32[]{:S(2)}, u32[]{:S(2)}) collective-permute-start(f32[4,128,128]{2,1,0:T(8,128)S(1)} %multiply_add_fusion.6), channel_id=1, source_target_pairs={{4,0},{8,4},{12,8},{5,1},{9,5},{13,9},{6,2},{10,6},{14,10},{7,3},{... | collective-permute-start | bytes 786440 | tf_op jit(solution)/shard_map/while/body/eval_jaxpr/ppermute | solution.py:18
  57.4 8.8 %collective-permute-done.1 = f32[4,128,128]{2,1,0:T(8,128)S(1)} collective-permute-done((f32[4,128,128]{2,1,0:T(8,128)S(1)}, f32[4,128,128]{2,1,0:T(8,128)S(1)}, u32[]{:S(2)}, u32[]{:S(2)}) %collective-permute-start.1) | collective-permute-done | bytes 262176 | tf_op jit(solution)/shard_map/while/body/eval_jaxpr/ppermute | solution.py:18
  66.3 1.3 %collective-permute-start.1 = (f32[4,128,128]{2,1,0:T(8,128)S(1)}, f32[4,128,128]{2,1,0:T(8,128)S(1)}, u32[]{:S(2)}, u32[]{:S(2)}) collective-permute-start(f32[4,128,128]{2,1,0:T(8,128)S(1)} %multiply_add_fusion.6), channel_id=1, source_target_pairs={{4,0},{8,4},{12,8},{5,1},{9,5},{13,9},{6,2},{10,6},{14,10},{7,3},{... | collective-permute-start | bytes 786440 | tf_op jit(solution)/shard_map/while/body/eval_jaxpr/ppermute | solution.py:18
  67.6 7.3 %collective-permute-done.1 = f32[4,128,128]{2,1,0:T(8,128)S(1)} collective-permute-done((f32[4,128,128]{2,1,0:T(8,128)S(1)}, f32[4,128,128]{2,1,0:T(8,128)S(1)}, u32[]{:S(2)}, u32[]{:S(2)}) %collective-permute-start.1) | collective-permute-done | bytes 262176 | tf_op jit(solution)/shard_map/while/body/eval_jaxpr/ppermute | solution.py:18
  74.9 0.8 multiply_reduce_fusion
  75.7 0.5 fusion.100
  76.2 0.1 copy.140
  76.3 0.5 fusion.33
  76.8 0.1 copy.141
  77.0 0.3 fusion.4
  77.3 0.6 fusion.79
  77.9 0.8 copy.145
  78.8 0.6 fusion.56
  79.4 0.1 copy.151
  79.5 0.4 fusion.75
  79.9 0.1 copy.149
  80.1 0.1 copy.167
  80.2 1.4 %fusion.98 = (f32[4,128]{1,0:T(4,128)S(1)}, bf16[1,128,4,128]{3,2,1,0:T(4,128)(2,1)S(1)}, bf16[1,128,4,128]{3,2,1,0:T(4,128)(2,1)S(1)}, f32[1,128,4,128]{3,2,1,0:T(4,128)S(1)}) fusion(f32[1,128,4,128]{3,2,1,0:T(4,128)S(1)} %fusion.9, f32[4,128]{1,0:T(4,128)S(1)} %slice_bitcast_fusion, f32[1,128,4,128]{3,2,1,0:T(4,128)S(1)} %copy.167, f32[128]{0:T(128)} %copy-done.9, ...), kind=kLoop, calls=%fused_computation.145 | loop fusion | flops 1048064 | bytes 2364416 | tf_op jit(solution)/shard_map/transpose(jvp())/reduce_sum | solution.py:51
  81.7 0.1 copy.168
  81.8 0.7 copy-done
  82.6 0.8 reshape.491
  83.4 2.9 %fusion.55 = (f32[4,128]{1,0:T(4,128)S(1)}, f32[1,128,4,128]{3,2,1,0:T(4,128)S(1)}) fusion(f32[128,4,128]{2,1,0:T(4,128)} %reshape.491, f32[4,128]{1,0:T(4,128)S(1)} %bitcast.191, f32[1,128,4,128]{3,2,1,0:T(4,128)S(1)} %copy.167, f32[4,128,128]{2,0,1:T(4,128)S(1)} %copy.151, f32[1,1,4,128]{3,2,1,0:T(4,128)S(1)} %bitcast_add_fusion.2, ...), kind=kOutput, calls=%fused_computation.89 | output fusion | flops 10354176 | bytes 2105856 | tf_op jit(solution)/shard_map/transpose(jvp(jit(cumsum)))/reduce_window_sum | solution.py:31
  86.3 0.6 copy-done.6
  87.0 0.3 fusion.87
  87.3 13.6 %all-reduce.1 = (f32[512]{0:T(512)S(1)}, f32[512]{0:T(512)S(1)}) all-reduce(f32[512]{0:T(512)S(1)} %negate_bitcast_fusion, f32[512]{0:T(512)S(1)} %bitcast.192), channel_id=1, replica_groups=mesh['groups'=2,'ctx'=4,'head'=2,'rep'=2] {'ctx','rep'}, use_global_device_ids=true, to_apply=%region_14.15 | all-reduce | flops 1024 | bytes 8192 | tf_op jit(solution)/shard_map/psum | solution.py:139
  100.9 0.6 broadcast_multiply_fusion.1
  101.6 0.9 fusion.15
  102.5 0.6 convolution_convert_fusion
  103.1 0.3 fusion.5
  103.4 0.8 copy.155
  104.1 0.7 convert_element_type.156
  104.9 0.7 convert_element_type.158
  (51 shorter events, 1.4 us)
Async XLA Ops:
  0.6 1.0 copy-start.7
  1.6 4.3 %copy-start.1 = (bf16[1,128,512]{2,1,0:T(8,128)(2,1)S(1)}, bf16[1,128,512]{2,1,0:T(8,128)(2,1)}, u32[]{:S(2)}) copy-start(bf16[1,128,512]{2,1,0:T(8,128)(2,1)} %param.14) | copy-start | bytes 393220
  2.0 0.7 copy-start.13
  6.0 1.1 %copy-start.9 = (f32[128]{0:T(128)}, f32[128]{0:T(128)S(1)}, u32[]{:S(2)}) copy-start(f32[128]{0:T(128)S(1)} %get-tuple-element.174) | copy-start | bytes 1540
  6.1 0.9 copy-start.2
  7.6 29.0 %copy-start.3 = (bf16[1,128,512]{2,1,0:T(8,128)(2,1)S(1)}, bf16[1,128,512]{2,1,0:T(8,128)(2,1)}, u32[]{:S(2)}) copy-start(bf16[1,128,512]{2,1,0:T(8,128)(2,1)} %param.13) | copy-start | bytes 393220
  7.8 10.5 %collective-permute-start = (f32[4,128,128]{2,1,0:T(8,128)S(1)}, f32[4,128,128]{2,1,0:T(8,128)S(1)}, u32[]{:S(2)}, u32[]{:S(2)}) collective-permute-start(f32[4,128,128]{2,1,0:T(8,128)S(1)} %multiply_add_fusion.5), channel_id=1, source_target_pairs={{0,4},{4,8},{8,12},{1,5},{5,9},{9,13},{2,6},{6,10},{10,14},{3,7},{... | collective-permute-start | bytes 786440 | tf_op jit(solution)/shard_map/while/body/eval_jaxpr/ppermute | solution.py:18
  18.4 9.1 %collective-permute-start = (f32[4,128,128]{2,1,0:T(8,128)S(1)}, f32[4,128,128]{2,1,0:T(8,128)S(1)}, u32[]{:S(2)}, u32[]{:S(2)}) collective-permute-start(f32[4,128,128]{2,1,0:T(8,128)S(1)} %multiply_add_fusion.5), channel_id=1, source_target_pairs={{0,4},{4,8},{8,12},{1,5},{5,9},{9,13},{2,6},{6,10},{10,14},{3,7},{... | collective-permute-start | bytes 786440 | tf_op jit(solution)/shard_map/while/body/eval_jaxpr/ppermute | solution.py:18
  27.6 8.3 %collective-permute-start = (f32[4,128,128]{2,1,0:T(8,128)S(1)}, f32[4,128,128]{2,1,0:T(8,128)S(1)}, u32[]{:S(2)}, u32[]{:S(2)}) collective-permute-start(f32[4,128,128]{2,1,0:T(8,128)S(1)} %multiply_add_fusion.5), channel_id=1, source_target_pairs={{0,4},{4,8},{8,12},{1,5},{5,9},{9,13},{2,6},{6,10},{10,14},{3,7},{... | collective-permute-start | bytes 786440 | tf_op jit(solution)/shard_map/while/body/eval_jaxpr/ppermute | solution.py:18
  39.3 0.7 copy-start.4
  40.2 5.0 %copy-start.14 = (f32[1,128]{1,0:T(1,128)S(1)}, f32[1,128]{1,0:T(1,128)}, u32[]{:S(2)}) copy-start(f32[1,128]{1,0:T(1,128)} %param.19) | copy-start | bytes 1540
  45.2 0.5 copy-start.15
  45.7 31.3 %copy-start.5 = (f32[128]{0:T(128)}, f32[128]{0:T(128)S(1)}, u32[]{:S(2)}) copy-start(f32[128]{0:T(128)S(1)} %bitcast_subtract_fusion.1) | copy-start | bytes 1540
  46.8 9.2 %collective-permute-start.1 = (f32[4,128,128]{2,1,0:T(8,128)S(1)}, f32[4,128,128]{2,1,0:T(8,128)S(1)}, u32[]{:S(2)}, u32[]{:S(2)}) collective-permute-start(f32[4,128,128]{2,1,0:T(8,128)S(1)} %multiply_add_fusion.6), channel_id=1, source_target_pairs={{4,0},{8,4},{12,8},{5,1},{9,5},{13,9},{6,2},{10,6},{14,10},{7,3},{... | collective-permute-start | bytes 786440 | tf_op jit(solution)/shard_map/while/body/eval_jaxpr/ppermute | solution.py:18
  56.1 10.1 %collective-permute-start.1 = (f32[4,128,128]{2,1,0:T(8,128)S(1)}, f32[4,128,128]{2,1,0:T(8,128)S(1)}, u32[]{:S(2)}, u32[]{:S(2)}) collective-permute-start(f32[4,128,128]{2,1,0:T(8,128)S(1)} %multiply_add_fusion.6), channel_id=1, source_target_pairs={{4,0},{8,4},{12,8},{5,1},{9,5},{13,9},{6,2},{10,6},{14,10},{7,3},{... | collective-permute-start | bytes 786440 | tf_op jit(solution)/shard_map/while/body/eval_jaxpr/ppermute | solution.py:18
  66.3 8.6 %collective-permute-start.1 = (f32[4,128,128]{2,1,0:T(8,128)S(1)}, f32[4,128,128]{2,1,0:T(8,128)S(1)}, u32[]{:S(2)}, u32[]{:S(2)}) collective-permute-start(f32[4,128,128]{2,1,0:T(8,128)S(1)} %multiply_add_fusion.6), channel_id=1, source_target_pairs={{4,0},{8,4},{12,8},{5,1},{9,5},{13,9},{6,2},{10,6},{14,10},{7,3},{... | collective-permute-start | bytes 786440 | tf_op jit(solution)/shard_map/while/body/eval_jaxpr/ppermute | solution.py:18
  80.2 1.4 %copy-start.11 = (f32[4,128]{1,0:T(4,128)S(1)}, f32[4,128]{1,0:T(4,128)}, u32[]{:S(2)}) copy-start(f32[4,128]{1,0:T(4,128)} %get-tuple-element.145) | copy-start | bytes 6148
  80.2 1.4 %copy-start.12 = (f32[4,128]{1,0:T(4,128)S(1)}, f32[4,128]{1,0:T(4,128)}, u32[]{:S(2)}) copy-start(f32[4,128]{1,0:T(4,128)} %get-tuple-element.146) | copy-start | bytes 6148
  81.7 0.9 copy-start
  82.6 0.8 copy-start.8
  82.6 0.8 copy-start.10
  86.3 0.7 copy-start.6
where the time goes:
time: 106 us
  waiting for transfers between devices  38 us (36%)
  blocking collectives  18.5 us (17%)
  starting transfers between devices  17.6 us (17%)
  local copies, waits for them, and re-layouts  11.5 us (11%)
  other arithmetic  9.63 us (9%)
  matrix products  7.78 us (7%)
  between operations  2.37 us (2%)
    ppermute x6, waiting for transfers between devices, from_behind(): return lax.ppermute(value, axis, pairs)  38 us
    ppermute x6, starting transfers between devices, from_behind(): return lax.ppermute(value, axis, pairs)  17.6 us
    psum x1, blocking collectives, on_device(): lax.psum((grad_bias.reshape(-1), grad_weight.reshape(-1)), ('ctx', 'rep'))  13.6 us
    unnamed x35, local copies, waits for them, and re-layouts  5.02 us
    psum x1, blocking collectives, on_device(): value_pred = lax.psum(partial_value, 'head')  4.94 us
    another operation x2, other arithmetic, block_pass(): jnp.cumsum(decay.reshape(blocks, block_len, head_count, channels), axis=1)  3.28 us
  transfers between devices with their start and end apart: 6, of which 6 were waited for; matrix products, arithmetic and copies ran while one was open for 0% of the time, Pallas kernels for 0%

commit v1 on v0

v1 whole, which is shorter than its diff:
```python
import functools

import jax
import jax.numpy as jnp
from jax import lax
from jax.experimental import pallas as pl
from jax.experimental.pallas import tpu as pltpu
from jax.sharding import PartitionSpec as P

DK = 128
DV = 128
EPSILON = 1.0
GATE_SCALE = 16.0
MESH = pl.DeviceIdType.MESH
f32 = jnp.float32
bf16 = jnp.bfloat16


def dot(a, b, da, db):
    return lax.dot_general(a, b, (((da,), (db,)), ((), ())), preferred_element_type=f32)


def split_dot(ones, x):
    hi = x.astype(bf16)
    lo = (x - hi.astype(f32)).astype(bf16)
    return dot(ones, hi, 1, 0) + dot(ones, lo, 1, 0)


def kernel(
    n_ctx, n_head, n_rep, heads,
    q_ref, k_ref, v_ref, g_ref, bias_ref, weight_ref, target_ref, kind_ref, start_ref,
    value_out, dq_out, dk_out, dv_out, dg_out, dbias_out, dweight_out,
    qd, kd, kt, vt, probs, e_up, e_down, slope, att, s_loc, s_in, g_dir, g_in,
    ptg, dqd, dkd, last, vals, red,
    s_send, s_recv, gs_send, gs_recv, v_send, v_recv, r_send, r_recv,
):
    T = q_ref.shape[1]
    ctx = lax.axis_index("ctx")
    head = lax.axis_index("head")
    rep = lax.axis_index("rep")
    n_red = n_ctx * n_rep
    me = ctx * n_rep + rep

    barrier = pltpu.get_barrier_semaphore()
    for o in range(1, n_red):
        to = lax.rem(me + o, n_red)
        pl.semaphore_signal(
            barrier, inc=1, device_id={"ctx": to // n_rep, "rep": lax.rem(to, n_rep)},
            device_id_type=MESH,
        )
    for o in range(1, n_head):
        pl.semaphore_signal(
            barrier, inc=1, device_id={"head": lax.rem(head + o, n_head)}, device_id_type=MESH
        )

    rows = lax.broadcasted_iota(jnp.int32, (T, T), 0)
    cols = lax.broadcasted_iota(jnp.int32, (T, T), 1)
    lower = (rows >= cols)
    lower_b = jnp.where(lower, 1.0, 0.0).astype(bf16)
    flags = start_ref[...].astype(f32)
    seg_col = jnp.sum(jnp.where(lower, flags, 0.0), axis=1, keepdims=True)
    seg_last = jnp.sum(flags, axis=1, keepdims=True)
    alive = jnp.where(seg_col == 0.0, 1.0, 0.0)
    tail = jnp.where(seg_col == seg_last, 1.0, 0.0)
    alive_last = jnp.where(seg_last == 0.0, 1.0, 0.0)

    def cut(h):
        return slice(h * DK, (h + 1) * DK)

    def state_copy(h):
        return pltpu.make_async_remote_copy(
            src_ref=s_loc.at[h], dst_ref=s_in.at[h], send_sem=s_send.at[h], recv_sem=s_recv.at[h],
            device_id={"ctx": lax.rem(ctx + 1, n_ctx)}, device_id_type=MESH,
        )

    def grad_copy(h):
        return pltpu.make_async_remote_copy(
            src_ref=g_dir.at[h], dst_ref=g_in.at[h], send_sem=gs_send.at[h], recv_sem=gs_recv.at[h],
            device_id={"ctx": lax.rem(ctx + n_ctx - 1, n_ctx)}, device_id_type=MESH,
        )

    for h in range(heads):
        x = g_ref[0, :, cut(h)].astype(f32) + bias_ref[:, cut(h)]
        e = jnp.exp(-jnp.abs(x))
        decay = (jnp.minimum(x, 0.0) - jnp.log(1.0 + e)) * (1.0 / GATE_SCALE)
        slope[h] = jnp.where(x >= 0.0, e, 1.0) / (1.0 + e) * (1.0 / GATE_SCALE)
        cum = split_dot(lower_b, decay)
        up = jnp.exp(cum)
        down = jnp.exp(-cum)
        e_up[h] = up * DK ** (-0.5)
        e_down[h] = down
        up_last = up[T - 1 : T, :]
        last[h : h + 1, :] = up_last
        k_dec = k_ref[0, :, cut(h)].astype(f32) * down
        kd[h] = k_dec.astype(bf16)
        tail_k = (k_dec * up_last * tail).astype(bf16)
        kt[h] = tail_k
        s_loc[h] = dot(v_ref[0, :, cut(h)], tail_k, 0, 0)

    pl.semaphore_wait(barrier, n_red + n_head - 2)

    @pl.when(ctx == 0)
    def _():
        if n_ctx > 1:
            for h in range(heads):
                state_copy(h).start()
        s_in[...] = jnp.zeros_like(s_in)

    eye = rows == cols
    start_col = jnp.sum(jnp.where(eye, flags, 0.0), axis=1, keepdims=True)
    seg_row = jnp.sum(jnp.where(rows <= cols, start_col, 0.0), axis=0, keepdims=True)
    kind = kind_ref[...]
    window = jnp.where(kind == 0, T, jnp.where(kind == 1, T // 2, jnp.where(kind == 2, T // 4, T // 8)))
    live = lower & (seg_col == seg_row) & (rows - cols < window)
    for h in range(heads):
        q_dec = (q_ref[0, :, cut(h)].astype(f32) * e_up[h]).astype(bf16)
        qd[h] = q_dec
        p = jnp.where(live, dot(q_dec, kd[h], 1, 1), 0.0).astype(bf16)
        probs[h] = p
        att[h] = dot(p, v_ref[0, :, cut(h)], 1, 0)
        vt[h] = (v_ref[0, :, cut(h)].astype(f32) * tail).astype(bf16)

    partial = jnp.zeros((T, 1), f32)
    for h in range(heads):
        if n_ctx > 1:
            @pl.when(ctx > 0)
            def _():
                state_copy(h).wait_recv()

            @pl.when((ctx > 0) & (ctx < n_ctx - 1))
            def _():
                s_loc[h] = s_in[h] * (last[h : h + 1, :] * alive_last) + s_loc[h]
                state_copy(h).start()

        a = att[h] + dot(qd[h], s_in[h].astype(bf16), 1, 1) * alive
        att[h] = a
        w = weight_ref[:, cut(h)]
        inv = lax.rsqrt(jnp.mean(a * a, axis=1, keepdims=True) + EPSILON)
        partial = partial + jnp.sum(a * w, axis=1, keepdims=True) * inv

    part_row = jnp.sum(jnp.where(eye, partial, 0.0), axis=0, keepdims=True)
    vals[head] = jnp.broadcast_to(part_row, (8, T))

    def value_copy(slot, to):
        return pltpu.make_async_remote_copy(
            src_ref=vals.at[slot], dst_ref=vals.at[slot], send_sem=v_send.at[to],
            recv_sem=v_recv.at[slot], device_id={"head": to}, device_id_type=MESH,
        )

    for o in range(1, n_head):
        value_copy(head, lax.rem(head + o, n_head)).start()
    for o in range(1, n_head):
        value_copy(lax.rem(head + o, n_head), lax.rem(head + o, n_head)).wait_recv()
    value_row = vals[0, 0:1, :]
    for o in range(1, n_head):
        value_row = value_row + vals[o, 0:1, :]
    value_out[...] = value_row
    res_row = value_row - target_ref[...]
    res = jnp.sum(jnp.where(eye, res_row, 0.0), axis=1, keepdims=True)

    for h in range(heads):
        a = att[h]
        w = weight_ref[:, cut(h)]
        inv = lax.rsqrt(jnp.mean(a * a, axis=1, keepdims=True) + EPSILON)
        aw = jnp.mean(a * w, axis=1, keepdims=True)
        ri = res * inv
        red[me, heads + h : heads + h + 1, :] = jnp.sum(a * ri, axis=0, keepdims=True)
        g = ri * (w - a * (inv * inv * aw))
        ga = (g * alive).astype(bf16)
        g_dir[h] = dot(ga, qd[h], 0, 0)
        if n_ctx > 1:
            @pl.when(ctx == n_ctx - 1)
            def _():
                grad_copy(h).start()
        att[h] = g
    if n_ctx == 1:
        g_in[...] = jnp.zeros_like(g_in)
    else:
        @pl.when(ctx == n_ctx - 1)
        def _():
            g_in[...] = jnp.zeros_like(g_in)

    for h in range(heads):
        g = att[h]
        gb = g.astype(bf16)
        ga = (g * alive).astype(bf16)
        dp = jnp.where(live, dot(gb, v_ref[0, :, cut(h)], 1, 1), 0.0).astype(bf16)
        dq_dec = dot(dp, kd[h], 1, 0) + dot(ga, s_in[h].astype(bf16), 1, 0)
        dq_out[0, :, cut(h)] = (dq_dec * e_up[h]).astype(bf16)
        dqd[h] = dq_dec * qd[h].astype(f32)
        dkd[h] = dot(dp, qd[h], 0, 0)
        ptg[h] = dot(probs[h], gb, 0, 0)

    upper_b = jnp.where(rows <= cols, 1.0, 0.0).astype(bf16)
    for h in range(heads):
        if n_ctx > 1:
            @pl.when(ctx < n_ctx - 1)
            def _():
                grad_copy(h).wait_recv()

            @pl.when((ctx > 0) & (ctx < n_ctx - 1))
            def _():
                g_dir[h] = g_in[h] * (last[h : h + 1, :] * alive_last) + g_dir[h]
                grad_copy(h).start()

        up_last = last[h : h + 1, :]
        gs = g_in[h]
        gsb = gs.astype(bf16)
        dv_out[0, :, cut(h)] = (ptg[h] + dot(kt[h], gsb, 1, 1)).astype(bf16)
        tk = dot(vt[h], gsb, 1, 0) * up_last
        k_dec = kd[h].astype(f32)
        dk_dec = dkd[h] + tk
        dk_out[0, :, cut(h)] = (dk_dec * e_down[h]).astype(bf16)
        d_last = jnp.sum(k_dec * tk, axis=0, keepdims=True) + (
            jnp.sum(s_in[h] * gs, axis=0, keepdims=True) * (up_last * alive_last)
        )
        d_cum = dqd[h] - k_dec * dk_dec
        dx = (split_dot(upper_b, d_cum) + d_last) * slope[h]
        dg_out[0, :, cut(h)] = dx.astype(bf16)
        red[me, h : h + 1, :] = jnp.sum(dx, axis=0, keepdims=True)

    def red_copy(slot, to):
        return pltpu.make_async_remote_copy(
            src_ref=red.at[slot], dst_ref=red.at[slot], send_sem=r_send.at[to],
            recv_sem=r_recv.at[slot],
            device_id={"ctx": to // n_rep, "rep": lax.rem(to, n_rep)}, device_id_type=MESH,
        )

    for o in range(1, n_red):
        red_copy(me, lax.rem(me + o, n_red)).start()
    for o in range(1, n_red):
        other = lax.rem(me + o, n_red)
        red_copy(other, other).wait_recv()
    total = red[0]
    for o in range(1, n_red):
        total = total + red[o]
    total = total * (1.0 / (T * n_red))
    for h in range(heads):
        dbias_out[:, cut(h)] = total[h : h + 1, :]
        dweight_out[:, cut(h)] = total[heads + h : heads + h + 1, :]

    for o in range(1, n_red):
        red_copy(me, lax.rem(me + o, n_red)).wait_send()
    for o in range(1, n_head):
        value_copy(head, lax.rem(head + o, n_head)).wait_send()
    if n_ctx > 1:
        for h in range(heads):
            @pl.when(ctx < n_ctx - 1)
            def _():
                state_copy(h).wait_send()

            @pl.when(ctx > 0)
            def _():
                grad_copy(h).wait_send()


def on_device(n_ctx, n_head, n_rep, *args):
    q, k, v, g, bias, weight, targets, kinds, starts = args
    T, width = q.shape[1], q.shape[2]
    heads = width // DK
    n_red = n_ctx * n_rep
    vm = pl.BlockSpec(memory_space=pltpu.VMEM)
    half = lambda: pltpu.VMEM((heads, T, DK), bf16)
    full = lambda: pltpu.VMEM((heads, T, DK), f32)
    sems = lambda n: pltpu.SemaphoreType.DMA((n,))
    row16 = jax.ShapeDtypeStruct((1, T, width), bf16)
    row = jax.ShapeDtypeStruct((1, width), f32)
    outs = pl.pallas_call(
        functools.partial(kernel, n_ctx, n_head, n_rep, heads),
        out_shape=(jax.ShapeDtypeStruct((1, T), f32), row16, row16, row16, row16, row, row),
        in_specs=[vm] * 9,
        out_specs=(vm,) * 7,
        scratch_shapes=[
            half(), half(), half(), half(), pltpu.VMEM((heads, T, T), bf16),
            full(), full(), full(), full(), full(), full(), full(), full(),
            full(), full(), full(), pltpu.VMEM((8, DK), f32),
            pltpu.VMEM((n_head, 8, T), f32), pltpu.VMEM((n_red, 2 * heads, DK), f32),
            sems(heads), sems(heads), sems(heads), sems(heads),
            sems(n_head), sems(n_head), sems(n_red), sems(n_red),
        ],
        compiler_params=pltpu.CompilerParams(
            collective_id=0, has_side_effects=True, vmem_limit_bytes=24 * 2**20
        ),
    )(q, k, v, g, bias.reshape(1, width), weight.reshape(1, width), targets, kinds, starts)
    value, dq, dk, dv, dg, dbias, dweight = outs
    return value, dq, dk, dv, dg, dbias.reshape(width), dweight.reshape(width)


def solution(mesh):
    rows = ("groups", "rep")
    full, tokens = P(rows, "ctx", "head"), P(rows, "ctx")
    sums = P(("groups", "head"))
    shape = mesh.shape
    return jax.shard_map(
        functools.partial(on_device, shape["ctx"], shape["head"], shape["rep"]),
        mesh=mesh,
        in_specs=(full, full, full, full, P("head"), P("head"), tokens, tokens, tokens),
        out_specs=(tokens, full, full, full, full, sums, sums),
        check_vma=False,
    )
```

time: 106 us -> 47.9 us (0.45)
  waiting for transfers between devices: 38 us -> 0 us
  Pallas kernels: 0 us -> 37.8 us
  blocking collectives: 18.5 us -> 0 us
  starting transfers between devices: 17.6 us -> 0 us
  other arithmetic: 9.63 us -> 0 us
  matrix products: 7.78 us -> 0 us
  local copies, waits for them, and re-layouts: 11.5 us -> 8.56 us
    ppermute x6 -> x0, waiting for transfers between devices: 38 us -> none  [from_behind(): return lax.ppermute(value, axis, pairs)]
    pallas_call x0 -> x1, Pallas kernels: none -> 37.8 us  [on_device(): pl.pallas_call(functools.partial(kernel, n_ctx, n_head, n_rep, heads), ou...]
    psum x2 -> x0, blocking collectives: 18.5 us -> none  [the longest x1 13.6 us: on_device(): lax.psum((grad_bias.reshape(-1), grad_weight.reshape(-1)), ('ctx', 'rep'))]
    ppermute x6 -> x0, starting transfers between devices: 17.6 us -> none  [from_behind(): return lax.ppermute(value, axis, pairs)]
    dot_general x15 -> x0, matrix products: 7.47 us -> none  [the longest x3 1.85 us: block_pass(): jnp.einsum('bihc,bjhc->bhij', query_dec, key_dec, precision=highest)]
    convert_element_type x8 -> x0, local copies, waits for them, and re-layouts: 3.74 us -> none  [the longest x2 1.77 us: local_terms(): logit_in.astype(jnp.float32) + bias_in]
    another operation x3 -> x0, other arithmetic: 3.59 us -> none  [the longest x2 3.28 us: block_pass(): jnp.cumsum(decay.reshape(blocks, block_len, head_count, channels), axis=1)]
    unnamed x35 -> x23, local copies, waits for them, and re-layouts: 5.02 us -> 8.56 us
  transfers between devices with their start and end apart: 6 -> 0, of which waited for: 6 -> 0; matrix products, arithmetic and copies ran while one was open for 0% -> 0% of each run, Pallas kernels for 0% -> 0%
where the time goes in v1:
time: 47.9 us; the launch traced here: 47.7 us
  Pallas kernels  37.8 us (79%)
  local copies, waits for them, and re-layouts  8.56 us (18%)
  between operations  1.35 us (3%)
    pallas_call x1, Pallas kernels, on_device(): pl.pallas_call(functools.partial(kernel, n_ctx, n_head, n_rep, heads), ou...  37.8 us
    unnamed x23, local copies, waits for them, and re-layouts  8.56 us

profile of v1, /device:TPU:0, one launch (start us, length us, event | category | flops | bytes accessed | tf_op | source)
XLA Modules:
  0.0 47.7 jit_solution(10802048086753063760)
XLA Ops:
  0.6 0.0 copy-start.5
  1.3 0.0 copy-start.4
  1.3 0.0 copy-start.6
  1.3 0.0 copy-start.7
  1.3 0.0 copy-done.5
  1.3 0.6 %copy-done.4 = f32[512]{0:T(512)S(1)} copy-done((f32[512]{0:T(512)S(1)}, f32[512]{0:T(512)}, u32[]{:S(2)}) %copy-start.4) | copy-done | bytes 2072
  2.0 0.0 copy-done.6
  2.0 0.0 copy-done.7
  2.0 0.0 copy-start
  2.0 0.9 %copy-done = bf16[1,128,512]{2,1,0:T(8,128)(2,1)S(1)} copy-done((bf16[1,128,512]{2,1,0:T(8,128)(2,1)S(1)}, bf16[1,128,512]{2,1,0:T(8,128)(2,1)}, u32[]{:S(2)}) %copy-start) | copy-done | bytes 131096
  2.9 0.0 copy-start.1
  2.9 0.9 %copy-done.1 = bf16[1,128,512]{2,1,0:T(8,128)(2,1)S(1)} copy-done((bf16[1,128,512]{2,1,0:T(8,128)(2,1)S(1)}, bf16[1,128,512]{2,1,0:T(8,128)(2,1)}, u32[]{:S(2)}) %copy-start.1) | copy-done | bytes 131096
  3.8 0.0 copy-start.2
  3.8 0.9 %copy-done.2 = bf16[1,128,512]{2,1,0:T(8,128)(2,1)S(1)} copy-done((bf16[1,128,512]{2,1,0:T(8,128)(2,1)S(1)}, bf16[1,128,512]{2,1,0:T(8,128)(2,1)}, u32[]{:S(2)}) %copy-start.2) | copy-done | bytes 131096
  4.7 0.0 copy-start.3
  4.7 0.9 %copy-done.3 = bf16[1,128,512]{2,1,0:T(8,128)(2,1)S(1)} copy-done((bf16[1,128,512]{2,1,0:T(8,128)(2,1)S(1)}, bf16[1,128,512]{2,1,0:T(8,128)(2,1)}, u32[]{:S(2)}) %copy-start.3) | copy-done | bytes 131096
  5.6 37.8 %shard_map.144 = (f32[1,128]{1,0:T(1,128)S(1)}, bf16[1,128,512]{2,1,0:T(8,128)(2,1)S(1)}, bf16[1,128,512]{2,1,0:T(8,128)(2,1)S(1)}, bf16[1,128,512]{2,1,0:T(8,12...) custom-call(bf16[1,128,512]{2,1,0:T(8,128)(2,1)S(1)} %copy-done, ...), custom_call_target="tpu_custom_call" | custom-call | tf_op jit(solution)/shard_map/pallas_call | solution.py:268
  43.4 0.5 %copy.24 = f32[1,128]{1,0:T(1,128)} copy(f32[1,128]{1,0:T(1,128)S(1)} %get-tuple-element.28) | data formatting | bytes 1024
  43.9 0.7 %copy.25 = bf16[1,128,512]{2,1,0:T(8,128)(2,1)} copy(bf16[1,128,512]{2,1,0:T(8,128)(2,1)S(1)} %get-tuple-element.29) | data formatting | bytes 262144
  44.6 0.7 %copy.26 = bf16[1,128,512]{2,1,0:T(8,128)(2,1)} copy(bf16[1,128,512]{2,1,0:T(8,128)(2,1)S(1)} %get-tuple-element.30) | data formatting | bytes 262144
  45.2 0.7 %copy.27 = bf16[1,128,512]{2,1,0:T(8,128)(2,1)} copy(bf16[1,128,512]{2,1,0:T(8,128)(2,1)S(1)} %get-tuple-element.31) | data formatting | bytes 262144
  45.9 0.7 %copy.28 = bf16[1,128,512]{2,1,0:T(8,128)(2,1)} copy(bf16[1,128,512]{2,1,0:T(8,128)(2,1)S(1)} %get-tuple-element.32) | data formatting | bytes 262144
  46.5 0.6 %copy.29 = f32[512]{0:T(512)} copy(f32[512]{0:T(512)S(1)} %bitcast.7) | data formatting | bytes 4096
  47.1 0.6 %copy.30 = f32[512]{0:T(512)} copy(f32[512]{0:T(512)S(1)} %bitcast.6) | data formatting | bytes 4096
Async XLA Ops:
  0.6 0.7 %copy-start.5 = (f32[512]{0:T(512)S(1)}, f32[512]{0:T(512)}, u32[]{:S(2)}) copy-start(f32[512]{0:T(512)} %param.14) | copy-start | bytes 6148
  1.3 0.7 %copy-start.4 = (f32[512]{0:T(512)S(1)}, f32[512]{0:T(512)}, u32[]{:S(2)}) copy-start(f32[512]{0:T(512)} %param.13) | copy-start | bytes 6148
  1.3 0.7 %copy-start.6 = (f32[1,128]{1,0:T(1,128)S(1)}, f32[1,128]{1,0:T(1,128)}, u32[]{:S(2)}) copy-start(f32[1,128]{1,0:T(1,128)} %target_ref.1) | copy-start | bytes 1540
  1.3 0.7 %copy-start.7 = (s32[1,128]{1,0:T(1,128)S(1)}, s32[1,128]{1,0:T(1,128)}, u32[]{:S(2)}) copy-start(s32[1,128]{1,0:T(1,128)} %start_ref.1) | copy-start | bytes 1540
  2.0 0.9 %copy-start = (bf16[1,128,512]{2,1,0:T(8,128)(2,1)S(1)}, bf16[1,128,512]{2,1,0:T(8,128)(2,1)}, u32[]{:S(2)}) copy-start(bf16[1,128,512]{2,1,0:T(8,128)(2,1)} %q_ref.1) | copy-start | bytes 393220
  2.9 0.9 %copy-start.1 = (bf16[1,128,512]{2,1,0:T(8,128)(2,1)S(1)}, bf16[1,128,512]{2,1,0:T(8,128)(2,1)}, u32[]{:S(2)}) copy-start(bf16[1,128,512]{2,1,0:T(8,128)(2,1)} %k_ref.1) | copy-start | bytes 393220
  3.8 0.9 %copy-start.2 = (bf16[1,128,512]{2,1,0:T(8,128)(2,1)S(1)}, bf16[1,128,512]{2,1,0:T(8,128)(2,1)}, u32[]{:S(2)}) copy-start(bf16[1,128,512]{2,1,0:T(8,128)(2,1)} %v_ref.1) | copy-start | bytes 393220
  4.7 0.9 %copy-start.3 = (bf16[1,128,512]{2,1,0:T(8,128)(2,1)S(1)}, bf16[1,128,512]{2,1,0:T(8,128)(2,1)}, u32[]{:S(2)}) copy-start(bf16[1,128,512]{2,1,0:T(8,128)(2,1)} %g_ref.1) | copy-start | bytes 393220

commit v2 on v1

--- a/solution.py
+++ b/solution.py
@@ -9,6 +9,8 @@
 
 DK = 128
 DV = 128
+CUTS = 2
+ROWS = DV // CUTS
 EPSILON = 1.0
 GATE_SCALE = 16.0
 MESH = pl.DeviceIdType.MESH
@@ -28,13 +30,26 @@
 
 def kernel(
     n_ctx, n_head, n_rep, heads,
-    q_ref, k_ref, v_ref, g_ref, bias_ref, weight_ref, target_ref, kind_ref, start_ref,
-    value_out, dq_out, dk_out, dv_out, dg_out, dbias_out, dweight_out,
-    qd, kd, kt, vt, probs, e_up, e_down, slope, att, s_loc, s_in, g_dir, g_in,
-    ptg, dqd, dkd, last, vals, red,
-    s_send, s_recv, gs_send, gs_recv, v_send, v_recv, r_send, r_recv,
+    q_hbm, k_hbm, v_hbm, g_hbm, bias_hbm, weight_hbm, target_hbm, kind_hbm, start_hbm,
+    value_hbm, dq_hbm, dk_hbm, dv_hbm, dg_hbm, dbias_hbm, dweight_hbm,
+    q_ref, k_ref, v_ref, g_ref, bias_ref, weight_ref, target_ref, kind_ref, start_ref, loaded,
+    qd, kd, kt, vt, probs, e_up, e_down, slope, att, s_loc, s_pair, s_in, g_dir, g_pair, g_in,
+    ptg, dqd, dkd, last, pass_on, pair_pass, vals, red, dq_ref, dk_ref, dv_ref, dg_ref, rows_ref,
+    s_send, s_far, sp_recv, s_recv, g_send, g_far, gp_recv, g_recv, d_send, d_recv,
+    v_send, v_recv, r_send, r_recv, stored,
 ):
     T = q_ref.shape[1]
+    loads = {
+        name: pltpu.make_async_copy(src, dst, loaded.at[i])
+        for i, (name, src, dst) in enumerate((
+            ("gates", g_hbm, g_ref), ("bias", bias_hbm, bias_ref), ("starts", start_hbm, start_ref),
+            ("keys", k_hbm, k_ref), ("values", v_hbm, v_ref), ("queries", q_hbm, q_ref),
+            ("kinds", kind_hbm, kind_ref), ("weights", weight_hbm, weight_ref),
+            ("targets", target_hbm, target_ref),
+        ))
+    }
+    for load in loads.values():
+        load.start()
     ctx = lax.axis_index("ctx")
     head = lax.axis_index("head")
     rep = lax.axis_index("rep")
@@ -57,6 +72,7 @@
     cols = lax.broadcasted_iota(jnp.int32, (T, T), 1)
     lower = (rows >= cols)
     lower_b = jnp.where(lower, 1.0, 0.0).astype(bf16)
+    loads["starts"].wait()
     flags = start_ref[...].astype(f32)
     seg_col = jnp.sum(jnp.where(lower, flags, 0.0), axis=1, keepdims=True)
     seg_last = jnp.sum(flags, axis=1, keepdims=True)
@@ -67,18 +83,52 @@
     def cut(h):
         return slice(h * DK, (h + 1) * DK)
 
-    def state_copy(h):
+    pair, odd = ctx // 2, lax.rem(ctx, 2)
+    pairs = n_ctx // 2
+    first, final = pair == 0, pair == pairs - 1
+
+    def piece(ref, c):
+        return ref.at[c // CUTS, pl.ds(c % CUTS * ROWS, ROWS)]
+
+    def move(src, dst, c, send, recv, by):
         return pltpu.make_async_remote_copy(
-            src_ref=s_loc.at[h], dst_ref=s_in.at[h], send_sem=s_send.at[h], recv_sem=s_recv.at[h],
-            device_id={"ctx": lax.rem(ctx + 1, n_ctx)}, device_id_type=MESH,
-        )
-
-    def grad_copy(h):
-        return pltpu.make_async_remote_copy(
-            src_ref=g_dir.at[h], dst_ref=g_in.at[h], send_sem=gs_send.at[h], recv_sem=gs_recv.at[h],
-            device_id={"ctx": lax.rem(ctx + n_ctx - 1, n_ctx)}, device_id_type=MESH,
-        )
-
+            src_ref=piece(src, c), dst_ref=piece(dst, c), send_sem=send.at[c], recv_sem=recv.at[c],
+            device_id={"ctx": lax.rem(ctx + by + n_ctx, n_ctx)}, device_id_type=MESH,
+        )
+
+    def state_to_pair(c):
+        return move(s_loc, s_pair, c, s_send, sp_recv, 1)
+
+    def state_near(c):
+        return move(s_loc, s_in, c, s_send, s_recv, 1)
+
+    def state_far(c):
+        return move(s_loc, s_in, c, s_far, s_recv, 2)
+
+    def grad_to_pair(c):
+        return move(g_dir, g_pair, c, g_send, gp_recv, -1)
+
+    def grad_near(c):
+        return move(g_dir, g_in, c, g_send, g_recv, -1)
+
+    def grad_far(c):
+        return move(g_dir, g_in, c, g_far, g_recv, -2)
+
+    def of_head(h):
+        return range(h * CUTS, (h + 1) * CUTS)
+
+    pieces = range(heads * CUTS)
+    pass_copy = pltpu.make_async_remote_copy(
+        src_ref=pass_on, dst_ref=pair_pass, send_sem=d_send.at[0], recv_sem=d_recv.at[0],
+        device_id={"ctx": ctx + 1 - 2 * odd}, device_id_type=MESH,
+    )
+
+    def store(i, src, dst):
+        return pltpu.make_async_copy(src, dst, stored.at[i])
+
+    pass_on[...] = jnp.zeros_like(pass_on)
+    for name in ("gates", "bias", "keys", "values"):
+        loads[name].wait()
     for h in range(heads):
         x = g_ref[0, :, cut(h)].astype(f32) + bias_ref[:, cut(h)]
         e = jnp.exp(-jnp.abs(x))
@@ -91,6 +141,7 @@
         e_down[h] = down
         up_last = up[T - 1 : T, :]
         last[h : h + 1, :] = up_last
+        pass_on[h : h + 1, :] = up_last * alive_last
         k_dec = k_ref[0, :, cut(h)].astype(f32) * down
         kd[h] = k_dec.astype(bf16)
         tail_k = (k_dec * up_last * tail).astype(bf16)
@@ -99,13 +150,19 @@
 
     pl.semaphore_wait(barrier, n_red + n_head - 2)
 
+    @pl.when(odd == 0)
+    def _():
+        for c in pieces:
+            state_to_pair(c).start()
+
     @pl.when(ctx == 0)
     def _():
-        if n_ctx > 1:
-            for h in range(heads):
-                state_copy(h).start()
         s_in[...] = jnp.zeros_like(s_in)
 
+    pass_copy.start()
+
+    for name in ("queries", "kinds", "weights", "targets"):
+        loads[name].wait()
     eye = rows == cols
     start_col = jnp.sum(jnp.where(eye, flags, 0.0), axis=1, keepdims=True)
     seg_row = jnp.sum(jnp.where(rows <= cols, start_col, 0.0), axis=0, keepdims=True)
@@ -121,16 +178,36 @@
         vt[h] = (v_ref[0, :, cut(h)].astype(f32) * tail).astype(bf16)
 
     partial = jnp.zeros((T, 1), f32)
-    for h in range(heads):
-        if n_ctx > 1:
-            @pl.when(ctx > 0)
-            def _():
-                state_copy(h).wait_recv()
-
-            @pl.when((ctx > 0) & (ctx < n_ctx - 1))
-            def _():
-                s_loc[h] = s_in[h] * (last[h : h + 1, :] * alive_last) + s_loc[h]
-                state_copy(h).start()
+    pass_copy.wait_recv()
+    for h in range(heads):
+        for c in of_head(h):
+            part = (h, slice(c % CUTS * ROWS, (c % CUTS + 1) * ROWS))
+
+            @pl.when((odd == 0) & ~first)
+            def _():
+                state_near(c).wait_recv()
+
+            @pl.when((odd == 1) & first)
+            def _():
+                state_to_pair(c).wait_recv()
+                s_in[part] = s_pair[part]
+
+            @pl.when((odd == 1) & ~first)
+            def _():
+                state_to_pair(c).wait_recv()
+                state_far(c).wait_recv()
+                s_in[part] = s_in[part] * pair_pass[h : h + 1, :] + s_pair[part]
+
+            @pl.when((odd == 1) & ~final)
+            def _():
+                s_loc[part] = s_in[part] * pass_on[h : h + 1, :] + s_loc[part]
+                state_far(c).start()
+
+        if h == heads - 1:
+            @pl.when((odd == 1) & ~final)
+            def _():
+                for c in pieces:
+                    state_near(c).start()
 
         a = att[h] + dot(qd[h], s_in[h].astype(bf16), 1, 1) * alive
         att[h] = a
@@ -154,7 +231,9 @@
     value_row = vals[0, 0:1, :]
     for o in range(1, n_head):
         value_row = value_row + vals[o, 0:1, :]
-    value_out[...] = value_row
+    rows_ref[0, :, 0:T] = value_row
+    value_store = store(0, rows_ref.at[0, :, pl.ds(0, T)], value_hbm)
+    value_store.start()
     res_row = value_row - target_ref[...]
     res = jnp.sum(jnp.where(eye, res_row, 0.0), axis=1, keepdims=True)
 
@@ -168,17 +247,16 @@
         g = ri * (w - a * (inv * inv * aw))
         ga = (g * alive).astype(bf16)
         g_dir[h] = dot(ga, qd[h], 0, 0)
-        if n_ctx > 1:
-            @pl.when(ctx == n_ctx - 1)
-            def _():
-                grad_copy(h).start()
+        @pl.when(odd == 1)
+        def _():
+            for c in of_head(h):
+                grad_to_pair(c).start()
+
         att[h] = g
-    if n_ctx == 1:
+
+    @pl.when(ctx == n_ctx - 1)
+    def _():
         g_in[...] = jnp.zeros_like(g_in)
-    else:
-        @pl.when(ctx == n_ctx - 1)
-        def _():
-            g_in[...] = jnp.zeros_like(g_in)
 
     for h in range(heads):
         g = att[h]
@@ -186,38 +264,64 @@
         ga = (g * alive).astype(bf16)
         dp = jnp.where(live, dot(gb, v_ref[0, :, cut(h)], 1, 1), 0.0).astype(bf16)
         dq_dec = dot(dp, kd[h], 1, 0) + dot(ga, s_in[h].astype(bf16), 1, 0)
-        dq_out[0, :, cut(h)] = (dq_dec * e_up[h]).astype(bf16)
+        dq_ref[0, :, cut(h)] = (dq_dec * e_up[h]).astype(bf16)
         dqd[h] = dq_dec * qd[h].astype(f32)
         dkd[h] = dot(dp, qd[h], 0, 0)
         ptg[h] = dot(probs[h], gb, 0, 0)
 
+    stores = [value_store, store(1, dq_ref, dq_hbm)]
+    stores[1].start()
+
     upper_b = jnp.where(rows <= cols, 1.0, 0.0).astype(bf16)
     for h in range(heads):
-        if n_ctx > 1:
-            @pl.when(ctx < n_ctx - 1)
-            def _():
-                grad_copy(h).wait_recv()
-
-            @pl.when((ctx > 0) & (ctx < n_ctx - 1))
-            def _():
-                g_dir[h] = g_in[h] * (last[h : h + 1, :] * alive_last) + g_dir[h]
-                grad_copy(h).start()
+        for c in of_head(h):
+            part = (h, slice(c % CUTS * ROWS, (c % CUTS + 1) * ROWS))
+
+            @pl.when((odd == 1) & ~final)
+            def _():
+                grad_near(c).wait_recv()
+
+            @pl.when((odd == 0) & final)
+            def _():
+                grad_to_pair(c).wait_recv()
+                g_in[part] = g_pair[part]
+
+            @pl.when((odd == 0) & ~final)
+            def _():
+                grad_to_pair(c).wait_recv()
+                grad_far(c).wait_recv()
+                g_in[part] = g_in[part] * pair_pass[h : h + 1, :] + g_pair[part]
+
+            @pl.when((odd == 0) & ~first)
+            def _():
+                g_dir[part] = g_in[part] * pass_on[h : h + 1, :] + g_dir[part]
+                grad_far(c).start()
+
+        if h == heads - 1:
+            @pl.when((odd == 0) & ~first)
+            def _():
+                for c in pieces:
+                    grad_near(c).start()
 
         up_last = last[h : h + 1, :]
         gs = g_in[h]
         gsb = gs.astype(bf16)
-        dv_out[0, :, cut(h)] = (ptg[h] + dot(kt[h], gsb, 1, 1)).astype(bf16)
+        dv_ref[0, :, cut(h)] = (ptg[h] + dot(kt[h], gsb, 1, 1)).astype(bf16)
         tk = dot(vt[h], gsb, 1, 0) * up_last
         k_dec = kd[h].astype(f32)
         dk_dec = dkd[h] + tk
-        dk_out[0, :, cut(h)] = (dk_dec * e_down[h]).astype(bf16)
+        dk_ref[0, :, cut(h)] = (dk_dec * e_down[h]).astype(bf16)
         d_last = jnp.sum(k_dec * tk, axis=0, keepdims=True) + (
             jnp.sum(s_in[h] * gs, axis=0, keepdims=True) * (up_last * alive_last)
         )
         d_cum = dqd[h] - k_dec * dk_dec
         dx = (split_dot(upper_b, d_cum) + d_last) * slope[h]
-        dg_out[0, :, cut(h)] = dx.astype(bf16)
+        dg_ref[0, :, cut(h)] = dx.astype(bf16)
         red[me, h : h + 1, :] = jnp.sum(dx, axis=0, keepdims=True)
+
+    for i, src, dst in ((2, dk_ref, dk_hbm), (3, dv_ref, dv_hbm), (4, dg_ref, dg_hbm)):
+        stores.append(store(i, src, dst))
+        stores[-1].start()
 
     def red_copy(slot, to):
         return pltpu.make_async_remote_copy(
@@ -236,22 +340,52 @@
         total = total + red[o]
     total = total * (1.0 / (T * n_red))
     for h in range(heads):
-        dbias_out[:, cut(h)] = total[h : h + 1, :]
-        dweight_out[:, cut(h)] = total[heads + h : heads + h + 1, :]
+        rows_ref[1, :, cut(h)] = total[h : h + 1, :]
+        rows_ref[2, :, cut(h)] = total[heads + h : heads + h + 1, :]
+
+    for i, dst in ((5, dbias_hbm), (6, dweight_hbm)):
+        stores.append(store(i, rows_ref.at[i - 4], dst))
+        stores[-1].start()
 
     for o in range(1, n_red):
         red_copy(me, lax.rem(me + o, n_red)).wait_send()
     for o in range(1, n_head):
         value_copy(head, lax.rem(head + o, n_head)).wait_send()
-    if n_ctx > 1:
-        for h in range(heads):
-            @pl.when(ctx < n_ctx - 1)
-            def _():
-                state_copy(h).wait_send()
-
-            @pl.when(ctx > 0)
-            def _():
-                grad_copy(h).wait_send()
+    pass_copy.wait_send()
+
+    @pl.when((odd == 0) | ~final)
+    def _():
+        for c in pieces:
+            state_near(c).wait_send()
+
+    @pl.when((odd == 1) & ~final)
+    def _():
+        for c in pieces:
+            state_far(c).wait_send()
+
+    @pl.when((odd == 1) | ~first)
+    def _():
+        for c in pieces:
+            grad_near(c).wait_send()
+
+    @pl.when((odd == 0) & ~first)
+    def _():
+        for c in pieces:
+            grad_far(c).wait_send()
+
+    for copy in stores:
+        copy.wait()
+
+
+def hand_on(*refs):
+    count = len(refs) // 2
+    copies = [
+        pltpu.make_async_copy(refs[i], refs[count + i], refs[-1].at[i]) for i in range(count)
+    ]
+    for copy in copies:
+        copy.start()
+    for copy in copies:
+        copy.wait()
 
 
 def on_device(n_ctx, n_head, n_rep, *args):
@@ -259,29 +393,40 @@
     T, width = q.shape[1], q.shape[2]
     heads = width // DK
     n_red = n_ctx * n_rep
-    vm = pl.BlockSpec(memory_space=pltpu.VMEM)
+    hbm = pl.BlockSpec(memory_space=pltpu.HBM)
     half = lambda: pltpu.VMEM((heads, T, DK), bf16)
     full = lambda: pltpu.VMEM((heads, T, DK), f32)
     sems = lambda n: pltpu.SemaphoreType.DMA((n,))
     row16 = jax.ShapeDtypeStruct((1, T, width), bf16)
     row = jax.ShapeDtypeStruct((1, width), f32)
+    ins = (q, k, v, g, bias.reshape(1, width), weight.reshape(1, width), targets, kinds, starts)
+    shapes = (jax.ShapeDtypeStruct((1, T), f32), row16, row16, row16, row16, row, row)
     outs = pl.pallas_call(
         functools.partial(kernel, n_ctx, n_head, n_rep, heads),
-        out_shape=(jax.ShapeDtypeStruct((1, T), f32), row16, row16, row16, row16, row, row),
-        in_specs=[vm] * 9,
-        out_specs=(vm,) * 7,
+        out_shape=shapes,
+        in_specs=[hbm] * 9,
+        out_specs=(hbm,) * 7,
         scratch_shapes=[
+            *(pltpu.VMEM(a.shape, a.dtype) for a in ins), sems(9),
             half(), half(), half(), half(), pltpu.VMEM((heads, T, T), bf16),
-            full(), full(), full(), full(), full(), full(), full(), full(),
-            full(), full(), full(), pltpu.VMEM((8, DK), f32),
+            *(full() for _ in range(13)), *(pltpu.VMEM((8, DK), f32) for _ in range(3)),
             pltpu.VMEM((n_head, 8, T), f32), pltpu.VMEM((n_red, 2 * heads, DK), f32),
-            sems(heads), sems(heads), sems(heads), sems(heads),
-            sems(n_head), sems(n_head), sems(n_red), sems(n_red),
+            *(pltpu.VMEM((1, T, width), bf16) for _ in range(4)), pltpu.VMEM((3, 1, width), f32),
+            *(sems(heads * CUTS) for _ in range(8)), sems(1), sems(1),
+            sems(n_head), sems(n_head), sems(n_red), sems(n_red), sems(7),
         ],
         compiler_params=pltpu.CompilerParams(
-            collective_id=0, has_side_effects=True, vmem_limit_bytes=24 * 2**20
+            collective_id=0, has_side_effects=True, vmem_limit_bytes=60 * 2**20
         ),
-    )(q, k, v, g, bias.reshape(1, width), weight.reshape(1, width), targets, kinds, starts)
+    )(*ins)
+    outs = pl.pallas_call(
+        hand_on,
+        out_shape=shapes,
+        in_specs=[hbm] * 7,
+        out_specs=(hbm,) * 7,
+        scratch_shapes=[sems(7)],
+        compiler_params=pltpu.CompilerParams(vmem_limit_bytes=60 * 2**20),
+    )(*outs)
     value, dq, dk, dv, dg, dbias, dweight = outs
     return value, dq, dk, dv, dg, dbias.reshape(width), dweight.reshape(width)
 

time: 47.9 us -> 65.9 us (1.38)
  Pallas kernels: 37.8 us -> 64.4 us
  local copies, waits for them, and re-layouts: 8.56 us -> 0 us
    pallas_call x0 -> x1, Pallas kernels: none -> 17.2 us  [on_device(): pl.pallas_call(hand_on, out_shape=shapes, in_specs=[hbm] * 7, out_specs=(...]
    pallas_call x1, Pallas kernels: 37.8 us -> 47.2 us  [on_device(): pl.pallas_call(functools.partial(kernel, n_ctx, n_head, n_rep, heads), ou...]
    unnamed x23 -> x0, local copies, waits for them, and re-layouts: 8.56 us -> none
where the time goes in v2:
time: 65.9 us; the launch traced here: 65.7 us
  Pallas kernels  64.4 us (98%)
  between operations  1.29 us (2%)
    pallas_call x1, Pallas kernels, on_device(): pl.pallas_call(functools.partial(kernel, n_ctx, n_head, n_rep, heads), ou...  47.2 us
    pallas_call x1, Pallas kernels, on_device(): pl.pallas_call(hand_on, out_shape=shapes, in_specs=[hbm] * 7, out_specs=(...  17.2 us

profile of v2, /device:TPU:0, one launch (start us, length us, event | category | flops | bytes accessed | tf_op | source)
XLA Modules:
  0.0 65.7 jit_solution(16813345801019215667)
XLA Ops:
  1.3 47.2 %shard_map.144 = (f32[1,128]{1,0:T(1,128)}, bf16[1,128,512]{2,1,0:T(8,128)(2,1)}, bf16[1,128,512]{2,1,0:T(8,128)(2,1)}, bf16[1,128,512]{2,1,0:T(8,128)(2,1)}, bf...) custom-call(bf16[1,128,512]{2,1,0:T(8,128)(2,1)} %q_hbm.1, bf16[1,128,512]{2,1,0:T(8,128)(2,1)} %k_hbm.1, ...), custom_call_target="tpu_custom_call" | custom-call | tf_op jit(solution)/shard_map/pallas_call | solution.py:404
  48.5 17.2 %shard_map.145 = (f32[1,128]{1,0:T(1,128)}, bf16[1,128,512]{2,1,0:T(8,128)(2,1)}, bf16[1,128,512]{2,1,0:T(8,128)(2,1)}, bf16[1,128,512]{2,1,0:T(8,128)(2,1)}, bf...) custom-call(f32[1,128]{1,0:T(1,128)} %get-tuple-element.21.refs_0_, ...), custom_call_target="tpu_custom_call" | custom-call | tf_op jit(solution)/shard_map/pallas_call | solution.py:422

commit v3 on v1

--- a/solution.py
+++ b/solution.py
@@ -9,6 +9,8 @@
 
 DK = 128
 DV = 128
+CUTS = 4
+ROWS = DV // CUTS
 EPSILON = 1.0
 GATE_SCALE = 16.0
 MESH = pl.DeviceIdType.MESH
@@ -28,13 +30,25 @@
 
 def kernel(
     n_ctx, n_head, n_rep, heads,
-    q_ref, k_ref, v_ref, g_ref, bias_ref, weight_ref, target_ref, kind_ref, start_ref,
+    q_hbm, k_hbm, v_hbm, g_hbm, bias_hbm, weight_hbm, target_hbm, kind_hbm, start_hbm,
     value_out, dq_out, dk_out, dv_out, dg_out, dbias_out, dweight_out,
+    q_ref, k_ref, v_ref, g_ref, bias_ref, weight_ref, target_ref, kind_ref, start_ref, loaded,
     qd, kd, kt, vt, probs, e_up, e_down, slope, att, s_loc, s_in, g_dir, g_in,
     ptg, dqd, dkd, last, vals, red,
     s_send, s_recv, gs_send, gs_recv, v_send, v_recv, r_send, r_recv,
 ):
     T = q_ref.shape[1]
+    loads = {
+        name: pltpu.make_async_copy(src, dst, loaded.at[i])
+        for i, (name, src, dst) in enumerate((
+            ("gates", g_hbm, g_ref), ("bias", bias_hbm, bias_ref), ("starts", start_hbm, start_ref),
+            ("keys", k_hbm, k_ref), ("values", v_hbm, v_ref), ("queries", q_hbm, q_ref),
+            ("kinds", kind_hbm, kind_ref), ("weights", weight_hbm, weight_ref),
+            ("targets", target_hbm, target_ref),
+        ))
+    }
+    for load in loads.values():
+        load.start()
     ctx = lax.axis_index("ctx")
     head = lax.axis_index("head")
     rep = lax.axis_index("rep")
@@ -57,6 +71,7 @@
     cols = lax.broadcasted_iota(jnp.int32, (T, T), 1)
     lower = (rows >= cols)
     lower_b = jnp.where(lower, 1.0, 0.0).astype(bf16)
+    loads["starts"].wait()
     flags = start_ref[...].astype(f32)
     seg_col = jnp.sum(jnp.where(lower, flags, 0.0), axis=1, keepdims=True)
     seg_last = jnp.sum(flags, axis=1, keepdims=True)
@@ -69,16 +84,18 @@
 
     def state_copy(h):
         return pltpu.make_async_remote_copy(
-            src_ref=s_loc.at[h], dst_ref=s_in.at[h], send_sem=s_send.at[h], recv_sem=s_recv.at[h],
+            src_ref=s_loc.at[h // CUTS, pl.ds(h % CUTS * ROWS, ROWS)], dst_ref=s_in.at[h // CUTS, pl.ds(h % CUTS * ROWS, ROWS)], send_sem=s_send.at[h], recv_sem=s_recv.at[h],
             device_id={"ctx": lax.rem(ctx + 1, n_ctx)}, device_id_type=MESH,
         )
 
     def grad_copy(h):
         return pltpu.make_async_remote_copy(
-            src_ref=g_dir.at[h], dst_ref=g_in.at[h], send_sem=gs_send.at[h], recv_sem=gs_recv.at[h],
+            src_ref=g_dir.at[h // CUTS, pl.ds(h % CUTS * ROWS, ROWS)], dst_ref=g_in.at[h // CUTS, pl.ds(h % CUTS * ROWS, ROWS)], send_sem=gs_send.at[h], recv_sem=gs_recv.at[h],
             device_id={"ctx": lax.rem(ctx + n_ctx - 1, n_ctx)}, device_id_type=MESH,
         )
 
+    for name in ("gates", "bias", "keys", "values"):
+        loads[name].wait()
     for h in range(heads):
         x = g_ref[0, :, cut(h)].astype(f32) + bias_ref[:, cut(h)]
         e = jnp.exp(-jnp.abs(x))
@@ -102,10 +119,12 @@
     @pl.when(ctx == 0)
     def _():
         if n_ctx > 1:
-            for h in range(heads):
-                state_copy(h).start()
+            for c in range(CUTS * heads):
+                state_copy(c).start()
         s_in[...] = jnp.zeros_like(s_in)
 
+    for name in ("queries", "kinds", "weights", "targets"):
+        loads[name].wait()
     eye = rows == cols
     start_col = jnp.sum(jnp.where(eye, flags, 0.0), axis=1, keepdims=True)
     seg_row = jnp.sum(jnp.where(rows <= cols, start_col, 0.0), axis=0, keepdims=True)
@@ -123,14 +142,17 @@
     partial = jnp.zeros((T, 1), f32)
     for h in range(heads):
         if n_ctx > 1:
-            @pl.when(ctx > 0)
-            def _():
-                state_copy(h).wait_recv()
-
-            @pl.when((ctx > 0) & (ctx < n_ctx - 1))
-            def _():
-                s_loc[h] = s_in[h] * (last[h : h + 1, :] * alive_last) + s_loc[h]
-                state_copy(h).start()
+            for c in range(h * CUTS, (h + 1) * CUTS):
+                part = (h, slice(c % CUTS * ROWS, (c % CUTS + 1) * ROWS))
+
+                @pl.when(ctx > 0)
+                def _():
+                    state_copy(c).wait_recv()
+
+                @pl.when((ctx > 0) & (ctx < n_ctx - 1))
+                def _():
+                    s_loc[part] = s_in[part] * (last[h : h + 1, :] * alive_last) + s_loc[part]
+                    state_copy(c).start()
 
         a = att[h] + dot(qd[h], s_in[h].astype(bf16), 1, 1) * alive
         att[h] = a
@@ -171,7 +193,8 @@
         if n_ctx > 1:
             @pl.when(ctx == n_ctx - 1)
             def _():
-                grad_copy(h).start()
+                for c in range(h * CUTS, (h + 1) * CUTS):
+                    grad_copy(c).start()
         att[h] = g
     if n_ctx == 1:
         g_in[...] = jnp.zeros_like(g_in)
@@ -194,14 +217,17 @@
     upper_b = jnp.where(rows <= cols, 1.0, 0.0).astype(bf16)
     for h in range(heads):
         if n_ctx > 1:
-            @pl.when(ctx < n_ctx - 1)
-            def _():
-                grad_copy(h).wait_recv()
-
-            @pl.when((ctx > 0) & (ctx < n_ctx - 1))
-            def _():
-                g_dir[h] = g_in[h] * (last[h : h + 1, :] * alive_last) + g_dir[h]
-                grad_copy(h).start()
+            for c in range(h * CUTS, (h + 1) * CUTS):
+                part = (h, slice(c % CUTS * ROWS, (c % CUTS + 1) * ROWS))
+
+                @pl.when(ctx < n_ctx - 1)
+                def _():
+                    grad_copy(c).wait_recv()
+
+                @pl.when((ctx > 0) & (ctx < n_ctx - 1))
+                def _():
+                    g_dir[part] = g_in[part] * (last[h : h + 1, :] * alive_last) + g_dir[part]
+                    grad_copy(c).start()
 
         up_last = last[h : h + 1, :]
         gs = g_in[h]
@@ -244,7 +270,7 @@
     for o in range(1, n_head):
         value_copy(head, lax.rem(head + o, n_head)).wait_send()
     if n_ctx > 1:
-        for h in range(heads):
+        for h in range(CUTS * heads):
             @pl.when(ctx < n_ctx - 1)
             def _():
                 state_copy(h).wait_send()
@@ -260,28 +286,32 @@
     heads = width // DK
     n_red = n_ctx * n_rep
     vm = pl.BlockSpec(memory_space=pltpu.VMEM)
+    hbm = pl.BlockSpec(memory_space=pltpu.HBM)
     half = lambda: pltpu.VMEM((heads, T, DK), bf16)
     full = lambda: pltpu.VMEM((heads, T, DK), f32)
     sems = lambda n: pltpu.SemaphoreType.DMA((n,))
     row16 = jax.ShapeDtypeStruct((1, T, width), bf16)
     row = jax.ShapeDtypeStruct((1, width), f32)
+    ins = (q, k, v, g, bias.reshape(1, width), weight.reshape(1, width), targets, kinds, starts)
+    shapes = (jax.ShapeDtypeStruct((1, T), f32), row16, row16, row16, row16, row, row)
     outs = pl.pallas_call(
         functools.partial(kernel, n_ctx, n_head, n_rep, heads),
-        out_shape=(jax.ShapeDtypeStruct((1, T), f32), row16, row16, row16, row16, row, row),
-        in_specs=[vm] * 9,
+        out_shape=shapes,
+        in_specs=[hbm] * 9,
         out_specs=(vm,) * 7,
         scratch_shapes=[
+            *(pltpu.VMEM(a.shape, a.dtype) for a in ins), sems(9),
             half(), half(), half(), half(), pltpu.VMEM((heads, T, T), bf16),
             full(), full(), full(), full(), full(), full(), full(), full(),
             full(), full(), full(), pltpu.VMEM((8, DK), f32),
             pltpu.VMEM((n_head, 8, T), f32), pltpu.VMEM((n_red, 2 * heads, DK), f32),
-            sems(heads), sems(heads), sems(heads), sems(heads),
+            *(sems(CUTS * heads) for _ in range(4)),
             sems(n_head), sems(n_head), sems(n_red), sems(n_red),
         ],
         compiler_params=pltpu.CompilerParams(
-            collective_id=0, has_side_effects=True, vmem_limit_bytes=24 * 2**20
+            collective_id=0, has_side_effects=True, vmem_limit_bytes=60 * 2**20
         ),
-    )(q, k, v, g, bias.reshape(1, width), weight.reshape(1, width), targets, kinds, starts)
+    )(*ins)
     value, dq, dk, dv, dg, dbias, dweight = outs
     return value, dq, dk, dv, dg, dbias.reshape(width), dweight.reshape(width)
 

time: 47.9 us -> 45 us (0.939)
  local copies, waits for them, and re-layouts: 8.56 us -> 6.55 us
  Pallas kernels: 37.8 us -> 36.8 us
    unnamed x23 -> x19, local copies, waits for them, and re-layouts: 8.56 us -> 6.55 us
    pallas_call x1, Pallas kernels: 37.8 us -> 36.8 us  [on_device(): pl.pallas_call(functools.partial(kernel, n_ctx, n_head, n_rep, heads), ou...]
where the time goes in v3:
time: 45 us; the launch traced here: 44.7 us
  Pallas kernels  36.8 us (82%)
  local copies, waits for them, and re-layouts  6.55 us (15%)
  between operations  1.31 us (3%)
    pallas_call x1, Pallas kernels, on_device(): pl.pallas_call(functools.partial(kernel, n_ctx, n_head, n_rep, heads), ou...  36.8 us
    unnamed x19, local copies, waits for them, and re-layouts  6.55 us

profile of v3, /device:TPU:0, one launch (start us, length us, event | category | flops | bytes accessed | tf_op | source)
XLA Modules:
  0.0 44.7 jit_solution(11428247080842564984)
XLA Ops:
  1.3 36.8 %shard_map.144 = (f32[1,128]{1,0:T(1,128)}, bf16[1,128,512]{2,1,0:T(8,128)(2,1)}, bf16[1,128,512]{2,1,0:T(8,128)(2,1)}, bf16[1,128,512]{2,1,0:T(8,128)(2,1)}, bf...) custom-call(bf16[1,128,512]{2,1,0:T(8,128)(2,1)} %q_hbm.1, bf16[1,128,512]{2,1,0:T(8,128)(2,1)} %k_hbm.1, ...), custom_call_target="tpu_custom_call" | custom-call | tf_op jit(solution)/shard_map/pallas_call | solution.py:297
  38.1 0.0 copy-start.5
  38.1 0.6 %copy-done.5 = f32[1,128]{1,0:T(1,128)S(1)} copy-done((f32[1,128]{1,0:T(1,128)S(1)}, f32[1,128]{1,0:T(1,128)}, u32[]{:S(2)}) %copy-start.5) | copy-done | bytes 536
  38.8 0.5 %copy.24 = f32[1,128]{1,0:T(1,128)} copy(f32[1,128]{1,0:T(1,128)S(1)} %copy-done.5) | data formatting | bytes 1024
  39.3 0.0 copy-start.2
  39.3 1.6 %copy.25 = bf16[1,128,512]{2,1,0:T(8,128)(2,1)} copy(bf16[1,128,512]{2,1,0:T(8,128)(2,1)} %get-tuple-element.29) | data formatting | bytes 262144
  40.9 0.0 copy-done.2
  40.9 0.0 copy-start.1
  40.9 0.7 %copy.26 = bf16[1,128,512]{2,1,0:T(8,128)(2,1)} copy(bf16[1,128,512]{2,1,0:T(8,128)(2,1)S(1)} %copy-done.2) | data formatting | bytes 262144
  41.6 0.3 copy-done.1
  41.9 0.0 copy-start
  41.9 0.7 %copy.27 = bf16[1,128,512]{2,1,0:T(8,128)(2,1)} copy(bf16[1,128,512]{2,1,0:T(8,128)(2,1)S(1)} %copy-done.1) | data formatting | bytes 262144
  42.5 0.3 copy-done
  42.8 0.0 copy-start.4
  42.8 0.7 %copy.28 = bf16[1,128,512]{2,1,0:T(8,128)(2,1)} copy(bf16[1,128,512]{2,1,0:T(8,128)(2,1)S(1)} %copy-done) | data formatting | bytes 262144
  43.5 0.0 copy-done.4
  43.5 0.0 copy-start.3
  43.5 0.6 %copy.29 = f32[512]{0:T(512)} copy(f32[512]{0:T(512)S(1)} %bitcast.7) | data formatting | bytes 4096
  44.1 0.1 copy-done.3
  44.1 0.6 %copy.30 = f32[512]{0:T(512)} copy(f32[512]{0:T(512)S(1)} %bitcast.6) | data formatting | bytes 4096
Async XLA Ops:
  38.1 0.7 %copy-start.5 = (f32[1,128]{1,0:T(1,128)S(1)}, f32[1,128]{1,0:T(1,128)}, u32[]{:S(2)}) copy-start(f32[1,128]{1,0:T(1,128)} %get-tuple-element.28) | copy-start | bytes 1540
  39.3 1.6 %copy-start.2 = (bf16[1,128,512]{2,1,0:T(8,128)(2,1)S(1)}, bf16[1,128,512]{2,1,0:T(8,128)(2,1)}, u32[]{:S(2)}) copy-start(bf16[1,128,512]{2,1,0:T(8,128)(2,1)} %get-tuple-element.30) | copy-start | bytes 393220
  40.9 1.0 %copy-start.1 = (bf16[1,128,512]{2,1,0:T(8,128)(2,1)S(1)}, bf16[1,128,512]{2,1,0:T(8,128)(2,1)}, u32[]{:S(2)}) copy-start(bf16[1,128,512]{2,1,0:T(8,128)(2,1)} %get-tuple-element.31) | copy-start | bytes 393220
  41.9 1.0 %copy-start = (bf16[1,128,512]{2,1,0:T(8,128)(2,1)S(1)}, bf16[1,128,512]{2,1,0:T(8,128)(2,1)}, u32[]{:S(2)}) copy-start(bf16[1,128,512]{2,1,0:T(8,128)(2,1)} %get-tuple-element.32) | copy-start | bytes 393220
  42.8 0.7 %copy-start.4 = (f32[1,512]{1,0:T(1,128)S(1)}, f32[1,512]{1,0:T(1,128)}, u32[]{:S(2)}) copy-start(f32[1,512]{1,0:T(1,128)} %get-tuple-element.19) | copy-start | bytes 6148
  43.5 0.6 %copy-start.3 = (f32[1,512]{1,0:T(1,128)S(1)}, f32[1,512]{1,0:T(1,128)}, u32[]{:S(2)}) copy-start(f32[1,512]{1,0:T(1,128)} %get-tuple-element.20) | copy-start | bytes 6148

commit v4 on v3

--- a/solution.py
+++ b/solution.py
@@ -309,7 +309,7 @@
             sems(n_head), sems(n_head), sems(n_red), sems(n_red),
         ],
         compiler_params=pltpu.CompilerParams(
-            collective_id=0, has_side_effects=True, vmem_limit_bytes=60 * 2**20
+            collective_id=0, has_side_effects=True, vmem_limit_bytes=54656 * 2**10
         ),
     )(*ins)
     value, dq, dk, dv, dg, dbias, dweight = outs

time: 45 us -> 42.5 us (0.944)
  local copies, waits for them, and re-layouts: 6.55 us -> 4.95 us
  Pallas kernels: 36.8 us -> 36 us
    unnamed x19 -> x15, local copies, waits for them, and re-layouts: 6.55 us -> 4.95 us
    pallas_call x1, Pallas kernels: 36.8 us -> 36 us  [on_device(): pl.pallas_call(functools.partial(kernel, n_ctx, n_head, n_rep, heads), ou...]
where the time goes in v4:
time: 42.5 us; the launch traced here: 42.3 us
  Pallas kernels  36 us (85%)
  local copies, waits for them, and re-layouts  4.95 us (12%)
  between operations  1.35 us (3%)
    pallas_call x1, Pallas kernels, on_device(): pl.pallas_call(functools.partial(kernel, n_ctx, n_head, n_rep, heads), ou...  36 us
    unnamed x15, local copies, waits for them, and re-layouts  4.95 us

profile of v4, /device:TPU:0, one launch (start us, length us, event | category | flops | bytes accessed | tf_op | source)
XLA Modules:
  0.0 42.3 jit_solution(11808798267348401673)
XLA Ops:
  0.6 0.0 copy-start.1
  1.3 0.0 copy-start
  1.3 0.0 copy-start.2
  1.3 0.0 copy-start.3
  1.3 0.0 copy-done.1
  1.3 0.6 %copy-done = f32[512]{0:T(512)S(1)} copy-done((f32[512]{0:T(512)S(1)}, f32[512]{0:T(512)}, u32[]{:S(2)}) %copy-start) | copy-done | bytes 2072
  2.0 0.0 copy-done.2
  2.0 0.0 copy-done.3
  2.0 36.0 %shard_map.144 = (f32[1,128]{1,0:T(1,128)S(1)}, bf16[1,128,512]{2,1,0:T(8,128)(2,1)S(1)}, bf16[1,128,512]{2,1,0:T(8,128)(2,1)S(1)}, bf16[1,128,512]{2,1,0:T(8,12...) custom-call(bf16[1,128,512]{2,1,0:T(8,128)(2,1)} %q_hbm.1, ...), custom_call_target="tpu_custom_call" | custom-call | tf_op jit(solution)/shard_map/pallas_call | solution.py:297
  38.0 0.5 %copy.24 = f32[1,128]{1,0:T(1,128)} copy(f32[1,128]{1,0:T(1,128)S(1)} %get-tuple-element.28) | data formatting | bytes 1024
  38.5 0.7 %copy.25 = bf16[1,128,512]{2,1,0:T(8,128)(2,1)} copy(bf16[1,128,512]{2,1,0:T(8,128)(2,1)S(1)} %get-tuple-element.29) | data formatting | bytes 262144
  39.2 0.7 %copy.26 = bf16[1,128,512]{2,1,0:T(8,128)(2,1)} copy(bf16[1,128,512]{2,1,0:T(8,128)(2,1)S(1)} %get-tuple-element.30) | data formatting | bytes 262144
  39.8 0.7 %copy.27 = bf16[1,128,512]{2,1,0:T(8,128)(2,1)} copy(bf16[1,128,512]{2,1,0:T(8,128)(2,1)S(1)} %get-tuple-element.31) | data formatting | bytes 262144
  40.5 0.7 %copy.28 = bf16[1,128,512]{2,1,0:T(8,128)(2,1)} copy(bf16[1,128,512]{2,1,0:T(8,128)(2,1)S(1)} %get-tuple-element.32) | data formatting | bytes 262144
  41.1 0.6 %copy.29 = f32[512]{0:T(512)} copy(f32[512]{0:T(512)S(1)} %bitcast.7) | data formatting | bytes 4096
  41.7 0.6 %copy.30 = f32[512]{0:T(512)} copy(f32[512]{0:T(512)S(1)} %bitcast.6) | data formatting | bytes 4096
Async XLA Ops:
  0.6 0.7 %copy-start.1 = (f32[512]{0:T(512)S(1)}, f32[512]{0:T(512)}, u32[]{:S(2)}) copy-start(f32[512]{0:T(512)} %param.14) | copy-start | bytes 6148
  1.3 0.7 %copy-start = (f32[512]{0:T(512)S(1)}, f32[512]{0:T(512)}, u32[]{:S(2)}) copy-start(f32[512]{0:T(512)} %param.13) | copy-start | bytes 6148
  1.3 0.7 %copy-start.2 = (f32[1,128]{1,0:T(1,128)S(1)}, f32[1,128]{1,0:T(1,128)}, u32[]{:S(2)}) copy-start(f32[1,128]{1,0:T(1,128)} %target_hbm.1) | copy-start | bytes 1540
  1.3 0.7 %copy-start.3 = (s32[1,128]{1,0:T(1,128)S(1)}, s32[1,128]{1,0:T(1,128)}, u32[]{:S(2)}) copy-start(s32[1,128]{1,0:T(1,128)} %start_hbm.1) | copy-start | bytes 1540
